TPU v7x, 32 devices: a whole 2x2x4 slice. The times are simulated.
32 devices in a mesh: expert: 4 (over y, core), tensor: 8 (over z, x).
Axes of the slice: x: 2, y: 2, z: 4, core: 2. Of those that a mesh axis runs over, the one named last changes fastest.
Arguments:
- tokens: bfloat16 [1024, 6144], P('expert', 'tensor'), may hold values from -6 to 6
- expert_ids: int32 [1024, 2], P('expert'), may hold values from 0 to 3, all different within a row; in each aligned block of 256 rows (0 to 255, 256 to 511, ...) at most 192 rows name the same one
- gate_prob: float32 [1024, 2], P('expert'), may hold values from 0.1 to 1
- w_gate: bfloat16 [4, 6144, 8192], P('expert', None, 'tensor'), may hold values from -0.078125 to 0.078125
- w_up: bfloat16 [4, 6144, 8192], P('expert', None, 'tensor'), may hold values from -0.078125 to 0.078125
- w_down: bfloat16 [4, 8192, 6144], P('expert', 'tensor'), may hold values from -0.09375 to 0.09375
Outputs:
- mixed: bfloat16 [1024, 6144], P('expert', 'tensor')
Inputs may be any that keep to these rules, and one draw needn't show every extreme that they name: `expert_ids`: the two experts of a row differ. Within the rows of one index of expert (aligned blocks of 256 rows) no expert is named by more than 192 rows, and in every draw some expert is named by exactly 192 rows of some block.
All inputs are finite; a program needn't handle non-finite values.
Results may differ from a plain program's by a relative error of at most 0.017.
Values may be sent and summed in bfloat16 or wider, within the bound.
A program may use at most 128 MiB of HBM per device.

v0:
```python
import jax
import jax.numpy as jnp
from jax import lax
from jax.sharding import PartitionSpec as P


def local(tokens, expert_ids, gate_prob, w_gate, w_up, w_down):
    experts = lax.axis_size("expert")
    me = lax.axis_index("expert")
    chips = experts // 2
    rows = tokens.shape[0]
    swap = [(e, e ^ 1) for e in range(experts)]
    across = [[2 * y + c for y in range(chips)] for c in range(2)]

    def weights(ids, prob):
        return jnp.sum(jnp.where(ids == me, prob, 0.0), axis=1)

    ids_all = lax.all_gather(expert_ids, "expert", axis=0)
    prob_all = lax.all_gather(gate_prob, "expert", axis=0)
    core = lax.rem(me, 2)
    ids_pair = ids_all.reshape(chips, 2, rows, 2)
    prob_pair = prob_all.reshape(chips, 2, rows, 2)

    def of_core(c):
        ids = lax.dynamic_index_in_dim(ids_pair, c, 1, keepdims=False)
        prob = lax.dynamic_index_in_dim(prob_pair, c, 1, keepdims=False)
        return weights(ids.reshape(chips * rows, 2), prob.reshape(chips * rows, 2))

    column = lax.all_gather(tokens, "expert", axis=0, tiled=True, axis_index_groups=across)
    mine = lax.all_gather(column, "tensor", axis=1, tiled=True)
    theirs = lax.ppermute(mine, "expert", swap)

    def ffn(x, weight):
        gate = jnp.dot(x, w_gate[0], preferred_element_type=jnp.float32)
        up = jnp.dot(x, w_up[0], preferred_element_type=jnp.float32)
        hidden = (jax.nn.silu(gate) * up).astype(jnp.bfloat16)
        out = jnp.dot(hidden, w_down[0], preferred_element_type=jnp.float32)
        return out * weight[:, None]

    part_mine = ffn(mine, of_core(core))
    part_theirs = ffn(theirs, of_core(1 - core)).astype(jnp.bfloat16)
    arrived = lax.ppermute(part_theirs, "expert", swap)
    total = (part_mine + arrived.astype(jnp.float32)).astype(jnp.bfloat16)
    summed = lax.psum_scatter(total, "tensor", scatter_dimension=1, tiled=True)
    out = lax.psum_scatter(
        summed.astype(jnp.float32).astype(jnp.bfloat16),
        "expert",
        scatter_dimension=0,
        tiled=True,
        axis_index_groups=across,
    )
    return out.astype(jnp.bfloat16)


def solution(mesh):
    return jax.shard_map(
        local,
        mesh=mesh,
        in_specs=(
            P("expert", "tensor"),
            P("expert", None),
            P("expert", None),
            P("expert", None, "tensor"),
            P("expert", None, "tensor"),
            P("expert", "tensor", None),
        ),
        out_specs=P("expert", "tensor"),
        check_vma=False,
    )
```

profile of v0, /device:TPU:11, one launch (start us, length us, event | category | flops | bytes accessed | tf_op | source)
XLA Modules:
  0.0 346.0 jit_solution(15449334686564308517)
XLA Ops:
  6.5 0.0 all-gather.4.cloned.1.call-start
  6.5 12.7 %all_gather.18 = bf16[512,768]{1,0:T(8,128)(2,1)} all-gather(bf16[256,768]{1,0:T(8,128)(2,1)} %param.6), channel_id=1, replica_groups={{0,16},{8,24},{1,17},{9,25},{2,18},{10,26},{3,19},{11,27},{4,20},{12,28..., dimensions={0}, use_global_device_ids=true | all-gather | bytes 1179648 | tf_op jit(solution)/shard_map/all_gather | solution.py:29
  19.3 0.0 all-gather.4.cloned.1.call-update
  19.3 0.0 reduce-scatter.3.cloned.1.call-start
  19.4 97.3 %all-gather.4.cloned.1.call-done = bf16[512,6144]{1,0:T(8,128)(2,1)} async-done(((bf16[512,768]{1,0:T(8,128)(2,1)}), bf16[512,6144]{1,0:T(8,128)(2,1)}) %all-gather.4.cloned.1.call-update) | async-done | bytes 6291472 | tf_op jit(solution)/shard_map/all_gather | solution.py:30
  116.7 1.7 collective-permute-start
  118.4 10.9 %all-gather = s32[1024,2]{0,1:T(2,128)S(1)} all-gather(s32[256,2]{0,1:T(2,128)} %param.7), channel_id=2, replica_groups=mesh['expert'=4,'tensor'=8] {'expert'}, dimensions={0}, use_global_device_ids=true | all-gather | bytes 10240 | tf_op jit(solution)/shard_map/all_gather | solution.py:18
  129.3 5.3 %all-gather.1 = f32[1024,2]{0,1:T(2,128)S(1)} all-gather(f32[256,2]{0,1:T(2,128)} %param.8), channel_id=3, replica_groups=mesh['expert'=4,'tensor'=8] {'expert'}, dimensions={0}, use_global_device_ids=true | all-gather | bytes 10240 | tf_op jit(solution)/shard_map/all_gather | solution.py:19
  134.7 0.0 collective-permute-done
  134.7 0.0 slice-start.3
  134.7 11.6 %fusion.4 = f32[512,1024]{1,0:T(8,128)S(1)} fusion(bf16[512,6144]{1,0:T(8,128)(2,1)} %collective-permute-done, bf16[1,6144,1024]{2,1,0:T(8,128)(2,1)} %param.10), kind=kOutput, calls=%fused_computation.4 | convolution fusion | flops 6442450944 | bytes 20971520 | tf_op jit(solution)/shard_map/dot_general | solution.py:35
  146.3 0.0 slice-start
  146.3 0.0 slice-start.1
  146.3 0.0 slice-start.4
  146.3 11.6 %fusion.8 = f32[512,1024]{1,0:T(8,128)S(1)} fusion(bf16[512,6144]{1,0:T(8,128)(2,1)} %collective-permute-done, bf16[1,6144,1024]{2,1,0:T(8,128)(2,1)} %param.9), kind=kOutput, calls=%fused_computation.8 | convolution fusion | flops 6442450944 | bytes 20971520 | tf_op jit(solution)/shard_map/dot_general | solution.py:34
  157.9 0.0 slice-start.2
  157.9 13.5 %multiply_convert_fusion = bf16[512,6144]{1,0:T(8,128)(2,1)} fusion(bf16[1,1024,6144]{2,1,0:T(8,128)(2,1)} %param.11, f32[512]{0:T(512)S(1)} %bitcast.37, f32[512,1024]{1,0:T(8,128)S(1)} %fusion.4, f32[512,1024]{1,0:T(8,128)S(1)} %fusion.8), kind=kOutput, calls=%fused_computation.13 | convolution fusion | flops 6451888128 | bytes 23070720 | tf_op jit(solution)/shard_map/dot_general | solution.py:37
  171.4 0.2 collective-permute-start.1
  171.6 0.0 slice-done.3
  171.6 0.0 slice-done
  171.6 0.0 slice-done.1
  171.6 0.0 slice-done.4
  171.6 0.0 slice-done.2
  171.7 6.7 %fusion.6 = f32[512,1024]{1,0:T(8,128)S(1)} fusion(bf16[512,6144]{1,0:T(8,128)(2,1)S(1)} %bitcast.41, bf16[1,6144,1024]{2,1,0:T(8,128)(2,1)S(1)} %bitcast.39), kind=kOutput, calls=%fused_computation.6 | convolution fusion | flops 6442450944 | bytes 20971520 | tf_op jit(solution)/shard_map/dot_general | solution.py:35
  178.4 10.2 %multiply_convert_fusion.2 = bf16[512,1024]{1,0:T(8,128)(2,1)S(1)} fusion(f32[512,1024]{1,0:T(8,128)S(1)} %fusion.6, bf16[512,6144]{1,0:T(8,128)(2,1)S(1)} %bitcast.41, bf16[1,6144,1024]{2,1,0:T(8,128)(2,1)} %param.9), kind=kOutput, calls=%fused_computation.15 | convolution fusion | flops 6445596672 | bytes 22020096 | tf_op jit(solution)/shard_map/dot_general | solution.py:34
  188.6 0.0 collective-permute-done.1
  188.6 14.3 %add_convert_fusion = bf16[512,6144]{1,0:T(8,128)(2,1)} fusion(bf16[512,6144]{1,0:T(8,128)(2,1)} %collective-permute-done.1, bf16[512,1024]{1,0:T(8,128)(2,1)S(1)} %multiply_convert_fusion.2, bf16[1,1024,6144]{2,1,0:T(8,128)(2,1)} %param.11, f32[512]{0:T(512)S(1)} %bitcast.36), kind=kOutput, calls=%fused_computation.12 | convolution fusion | flops 6455033856 | bytes 26216448 | tf_op jit(solution)/shard_map/dot_general | solution.py:37
  203.0 0.0 reduce-scatter.3.cloned.1.call-update
  203.0 0.0 reduce-scatter.5.cloned.1.call-start
  203.1 116.6 %reduce-scatter.3.cloned.1.call-done = bf16[512,768]{1,0:T(8,128)(2,1)} async-done(((bf16[512,6144]{1,0:T(8,128)(2,1)}), bf16[512,768]{1,0:T(8,128)(2,1)}) %reduce-scatter.3.cloned.1.call-update) | async-done | bytes 786448 | tf_op jit(solution)/shard_map/reduce_scatter | solution.py:44
  319.7 0.0 reduce-scatter.5.cloned.1.call-update
  319.7 19.7 %reduce-scatter.5.cloned.1.call-done = bf16[256,768]{1,0:T(8,128)(2,1)} async-done(((bf16[512,768]{1,0:T(8,128)(2,1)}), bf16[256,768]{1,0:T(8,128)(2,1)}) %reduce-scatter.5.cloned.1.call-update) | async-done | bytes 393232 | tf_op jit(solution)/shard_map/reduce_scatter | solution.py:45
  (7 shorter events, 0.1 us)
Async XLA Ops:
  6.5 110.1 %all-gather.4.cloned.1.call-start = ((), (), s32[]{:S(2)}) async-start(), calls=%async_computation.2 | async-start | bytes 7077888 | tf_op jit(solution)/shard_map/all_gather | solution.py:30
  19.3 300.4 %reduce-scatter.3.cloned.1.call-start = ((), (), s32[]{:S(2)}) async-start(), calls=%async_computation.3 | async-start | bytes 7077888 | tf_op jit(solution)/shard_map/reduce_scatter | solution.py:44
  116.7 18.0 %collective-permute-start = (bf16[512,6144]{1,0:T(8,128)(2,1)}, bf16[512,6144]{1,0:T(8,128)(2,1)}, u32[]{:S(2)}, u32[]{:S(2)}) collective-permute-start(bf16[512,6144]{1,0:T(8,128)(2,1)} %all-gather.4.cloned.1.call-done), channel_id=1, source_target_pairs={{0,8},{8,0},{16,24},{24,16},{1,9},{9,1},{17,25},{25,17},{2,10},{10... | collective-permute-start | bytes 18874376 | tf_op jit(solution)/shard_map/ppermute | solution.py:31
  134.7 36.9 %slice-start.3 = ((s8[6291456]{0:T(1024)(128)(4,1)}), s8[4194304]{0:T(1024)(128)(4,1)S(1)}, s32[]{:S(2)}) async-start(s8[6291456]{0:T(1024)(128)(4,1)} %bitcast.40), calls=%async_computation.8 | async-start | bytes 8388608
  146.3 25.3 %slice-start = ((s8[12582912]{0:T(1024)(128)(4,1)}), s8[4194304]{0:T(1024)(128)(4,1)S(1)}, s32[]{:S(2)}) async-start(s8[12582912]{0:T(1024)(128)(4,1)} %bitcast.38), calls=%async_computation.5 | async-start | bytes 8388608
  146.3 25.3 %slice-start.1 = ((s8[12582912]{0:T(1024)(128)(4,1)}), s8[4194304]{0:T(1024)(128)(4,1)S(1)}, s32[]{:S(2)}) async-start(s8[12582912]{0:T(1024)(128)(4,1)} %bitcast.38), calls=%async_computation.6 | async-start | bytes 8388608
  146.3 25.3 %slice-start.4 = ((s8[6291456]{0:T(1024)(128)(4,1)}), s8[2097152]{0:T(1024)(128)(4,1)S(1)}, s32[]{:S(2)}) async-start(s8[6291456]{0:T(1024)(128)(4,1)} %bitcast.40), calls=%async_computation.9 | async-start | bytes 4194304
  157.9 13.7 %slice-start.2 = ((s8[12582912]{0:T(1024)(128)(4,1)}), s8[4194304]{0:T(1024)(128)(4,1)S(1)}, s32[]{:S(2)}) async-start(s8[12582912]{0:T(1024)(128)(4,1)} %bitcast.38), calls=%async_computation.7 | async-start | bytes 8388608
  171.4 17.2 %collective-permute-start.1 = (bf16[512,6144]{1,0:T(8,128)(2,1)}, bf16[512,6144]{1,0:T(8,128)(2,1)}, u32[]{:S(2)}, u32[]{:S(2)}) collective-permute-start(bf16[512,6144]{1,0:T(8,128)(2,1)} %multiply_convert_fusion), channel_id=1, source_target_pairs={{0,8},{8,0},{16,24},{24,16},{1,9},{9,1},{17,25},{25,17},{2,10},{10... | collective-permute-start | bytes 18874376 | tf_op jit(solution)/shard_map/ppermute | solution.py:42
  203.0 136.4 %reduce-scatter.5.cloned.1.call-start = ((), (), s32[]{:S(2)}) async-start(), calls=%async_computation.4 | async-start | bytes 1179648 | tf_op jit(solution)/shard_map/reduce_scatter | solution.py:45
Sparse Core Ops, SparseCore 0:
  19.4 97.1 all-gather.3
  203.1 116.5 reduce-scatter.2
  321.9 17.4 reduce-scatter.4
where the time goes:
time: 348 us; the launch traced here: 346 us
  waiting for transfers between devices  234 us (67%)
  matrix products  68 us (20%)
  blocking collectives  28.9 us (8%)
  between operations  13.3 us (4%)
    reduce_scatter x1, waiting for transfers between devices, local(): summed = lax.psum_scatter(total, 'tensor', scatter_dimension=1, tiled=True)  117 us
    all_gather x1, waiting for transfers between devices, local(): mine = lax.all_gather(column, 'tensor', axis=1, tiled=True)  97.3 us
    dot_general x2, matrix products, ffn(): out = jnp.dot(hidden, w_down[0], preferred_element_type=jnp.float32)  27.8 us
    dot_general x2, matrix products, ffn(): gate = jnp.dot(x, w_gate[0], preferred_element_type=jnp.float32)  21.8 us
    reduce_scatter x1, waiting for transfers between devices, local(): lax.psum_scatter(summed.astype(jnp.float32).astype(jnp.bfloat16), 'expert...  19.7 us
    dot_general x2, matrix products, ffn(): up = jnp.dot(x, w_up[0], preferred_element_type=jnp.float32)  18.3 us
    all_gather x1, blocking collectives, local(): lax.all_gather(tokens, 'expert', axis=0, tiled=True, axis_index_groups=ac...  12.7 us
    all_gather x1, blocking collectives, local(): ids_all = lax.all_gather(expert_ids, 'expert', axis=0)  10.9 us
  transfers between devices with their start and end apart: 5, of which 3 were waited for; matrix products, arithmetic and copies ran while one was open for 5% of the time, Pallas kernels for 0%

commit v1 on v0

v1 whole, which is shorter than its diff:
```python
import functools

import jax
import jax.numpy as jnp
from jax import lax
from jax.experimental import pallas as pl
from jax.experimental.pallas import tpu as pltpu
from jax.sharding import PartitionSpec as P

MESH = pl.DeviceIdType.MESH
VMEM_LIMIT = 56 * 1024 * 1024


def place(nx, nz):
    e, t = lax.axis_index("expert"), lax.axis_index("tensor")
    y, core = e // 2, lax.rem(e, 2)
    z, x = t // nx, lax.rem(t, nx)
    return e, x, y, z, core


def greet(lines):
    barrier = pltpu.get_barrier_semaphore()
    for device in lines:
        pl.semaphore_signal(barrier, inc=1, device_id=device, device_id_type=MESH)
    pl.semaphore_wait(barrier, len(lines))


def remote(src, dst, sems, device):
    send, recv = sems
    return pltpu.make_async_remote_copy(
        src_ref=src,
        dst_ref=dst,
        send_sem=send,
        recv_sem=recv,
        device_id=device,
        device_id_type=MESH,
    )


def gather_kernel(
    nx, ny, nz, own_ref, aux_ref, g_ref, all_ref, s1, r1, s2, r2, s3, r3, sa, ra, local_sem
):
    e, x, y, z, core = place(nx, nz)
    experts = 2 * ny
    half = own_ref.shape[0] // 2
    t = z * nx + x

    def at_z(d):
        return (e, lax.rem(z + d, nz) * nx + x)

    def at_x(j):
        return (e, z * nx + lax.rem(x + j, nx))

    def at_y(j):
        return (lax.rem(y + j, ny) * 2 + core, t)

    def at_e(j):
        return (lax.rem(e + j, experts), t)

    greet(
        [at_z(d) for d in range(1, nz)]
        + [at_x(j) for j in range(1, nx)]
        + [at_e(j) for j in range(1, experts)]
    )
    waits = []
    rows = [pl.ds(0, half), pl.ds(half, half)]
    for h in range(2):
        keep = pltpu.make_async_copy(
            own_ref.at[rows[h]], g_ref.at[y, z, x, rows[h]], local_sem.at[h]
        )
        keep.start()
        waits.append((keep, False))
    first = {}
    for d in range(1, nz):
        for h in range(2):
            c = remote(
                own_ref.at[rows[h]],
                g_ref.at[y, z, x, rows[h]],
                (s1.at[h, d], r1.at[h, d]),
                at_z(d),
            )
            c.start()
            first[h, d] = c
    aux = []
    keep = pltpu.make_async_copy(aux_ref, all_ref.at[e], local_sem.at[2])
    keep.start()
    waits.append((keep, False))
    for j in range(1, experts):
        c = remote(aux_ref, all_ref.at[e], (sa.at[j], ra.at[j]), at_e(j))
        c.start()
        aux.append(c)

    second, third = {}, {}

    def forward(d):
        zs = lax.rem(z + nz - d, nz)
        for h in range(2):
            if d:
                first[h, d].wait_recv()
                src = g_ref.at[y, zs, x, rows[h]]
            else:
                src = own_ref.at[rows[h]]
            n, to = ((nx, at_x), (ny, at_y))[h]
            for j in range(1, n):
                c = remote(
                    src, g_ref.at[y, zs, x, rows[h]], (s2.at[h, d, j], r2.at[h, d, j]), to(j)
                )
                c.start()
                second[h, d, j] = c

    def spread(d):
        zs = lax.rem(z + nz - d, nz)
        for h in range(2):
            n, m, to = ((nx, ny, at_y), (ny, nx, at_x))[h]
            for j in range(1, n):
                second[h, d, j].wait_recv()
            if d == 0:
                waits[h][0].wait()
            slab = g_ref.at[y, zs, :, rows[h]] if h == 0 else g_ref.at[:, zs, x, rows[h]]
            for k in range(1, m):
                c = remote(slab, slab, (s3.at[h, d, k], r3.at[h, d, k]), to(k))
                c.start()
                third[h, d, k] = c

    forward(0)
    for d in range(1, nz):
        forward(d)
        spread(d - 1)
    spread(nz - 1)
    for c in third.values():
        c.wait_recv()
    for c in aux:
        c.wait()
    waits[2][0].wait()
    for c in [*first.values(), *second.values(), *third.values()]:
        c.wait_send()


def gather(tokens, aux, nx, ny, nz):
    rows, columns = tokens.shape
    n = max(nx, ny)
    dma = pltpu.SemaphoreType.DMA
    size = tokens.size * 2 * nx * ny * nz
    return pl.pallas_call(
        functools.partial(gather_kernel, nx, ny, nz),
        out_shape=(
            jax.ShapeDtypeStruct((ny, nz, nx, rows, columns), tokens.dtype),
            jax.ShapeDtypeStruct((2 * ny, *aux.shape), aux.dtype),
        ),
        in_specs=[pl.BlockSpec(memory_space=pl.ANY)] * 2,
        out_specs=[pl.BlockSpec(memory_space=pl.ANY)] * 2,
        scratch_shapes=[
            dma((2, nz)),
            dma((2, nz)),
            dma((2, nz, n)),
            dma((2, nz, n)),
            dma((2, nz, n)),
            dma((2, nz, n)),
            dma((2 * ny,)),
            dma((2 * ny,)),
            dma((3,)),
        ],
        cost_estimate=pl.CostEstimate(flops=0, bytes_accessed=2 * size, transcendentals=0),
        compiler_params=pltpu.CompilerParams(collective_id=0, has_side_effects=True),
    )(tokens, aux)


def reduce_kernel(
    nx, ny, nz, p_ref, o_ref, ya, xa, yb, xb, yc, xc, za, zb, s1, r1, s2, r2, s3, r3
):
    e, x, y, z, core = place(nx, nz)
    half = o_ref.shape[0] // 2
    t = z * nx + x
    f32 = jnp.float32

    def at_z(d):
        return (e, lax.rem(z + d, nz) * nx + x)

    def at_x(j):
        return (e, z * nx + lax.rem(x + j, nx))

    def at_y(j):
        return (lax.rem(y + j, ny) * 2 + core, t)

    greet(
        [at_z(d) for d in range(1, nz)]
        + [at_x(j) for j in range(1, nx)]
        + [at_y(j) for j in range(1, ny)]
    )
    rows = [pl.ds(0, half), pl.ds(half, half)]
    order = [*range(1, nz), 0]
    one, two, three = {}, {}, {}
    got, held, last = (ya, xa), (yb, xb), (yc, xc)
    for d in order:
        zt = lax.rem(z + d, nz)
        for h in range(2):
            n, to = ((ny, at_y), (nx, at_x))[h]
            for j in range(1, n):
                if h == 0:
                    src = p_ref.at[lax.rem(y + j, ny), zt, :, rows[h]]
                else:
                    src = p_ref.at[:, zt, lax.rem(x + j, nx), rows[h]]
                c = remote(src, got[h].at[d, j - 1], (s1.at[h, d, j], r1.at[h, d, j]), to(j))
                c.start()
                one[h, d, j] = c

    def middle(d):
        zt = lax.rem(z + d, nz)
        for h in range(2):
            n, m, to, at = ((ny, nx, at_x, x), (nx, ny, at_y, y))[h]
            for j in range(1, n):
                one[h, d, j].wait_recv()

            def add(i, _, h=h, n=n):
                if h == 0:
                    total = p_ref[y, zt, i, rows[h]].astype(f32)
                else:
                    total = p_ref[i, zt, x, rows[h]].astype(f32)
                for j in range(n - 1):
                    total += got[h][d, j, i].astype(f32)
                held[h][d, i] = total.astype(held[h].dtype)
                return 0

            lax.fori_loop(0, m, add, 0)
            for k in range(1, m):
                c = remote(
                    held[h].at[d, lax.rem(at + k, m)],
                    last[h].at[d, k - 1],
                    (s2.at[h, d, k], r2.at[h, d, k]),
                    to(k),
                )
                c.start()
                two[h, d, k] = c

    def end(d):
        for h in range(2):
            m, at = ((nx, x), (ny, y))[h]
            for k in range(1, m):
                two[h, d, k].wait_recv()
            total = held[h][d, at].astype(f32)
            for k in range(m - 1):
                total += last[h][d, k].astype(f32)
            za[h, d] = total.astype(za.dtype)
            if d:
                c = remote(za.at[h, d], zb.at[h, d - 1], (s3.at[h, d], r3.at[h, d]), at_z(d))
                c.start()
                three[h, d] = c

    for i, d in enumerate(order):
        middle(d)
        if i:
            end(order[i - 1])
    end(order[-1])
    for h in range(2):
        total = za[h, 0].astype(f32)
        for d in range(1, nz):
            three[h, d].wait_recv()
            total += zb[h, d - 1].astype(f32)
        o_ref[rows[h], :] = total.astype(o_ref.dtype)
    for c in [*one.values(), *two.values(), *three.values()]:
        c.wait_send()


def reduce_parts(parts, nx, ny, nz):
    rows, columns = parts.shape[-2:]
    half, n = rows // 2, max(nx, ny)
    kind = parts.dtype
    dma = pltpu.SemaphoreType.DMA
    return pl.pallas_call(
        functools.partial(reduce_kernel, nx, ny, nz),
        out_shape=jax.ShapeDtypeStruct((rows, columns), kind),
        in_specs=[pl.BlockSpec(memory_space=pltpu.VMEM)],
        out_specs=pl.BlockSpec(memory_space=pltpu.VMEM),
        scratch_shapes=[
            pltpu.VMEM((nz, ny - 1, nx, half, columns), kind),
            pltpu.VMEM((nz, nx - 1, ny, half, columns), kind),
            pltpu.VMEM((nz, nx, half, columns), kind),
            pltpu.VMEM((nz, ny, half, columns), kind),
            pltpu.VMEM((nz, nx - 1, half, columns), kind),
            pltpu.VMEM((nz, ny - 1, half, columns), kind),
            pltpu.VMEM((2, nz, half, columns), kind),
            pltpu.VMEM((2, nz - 1, half, columns), kind),
            dma((2, nz, n)),
            dma((2, nz, n)),
            dma((2, nz, n)),
            dma((2, nz, n)),
            dma((2, nz)),
            dma((2, nz)),
        ],
        cost_estimate=pl.CostEstimate(flops=0, bytes_accessed=4 * parts.size, transcendentals=0),
        compiler_params=pltpu.CompilerParams(
            collective_id=1, has_side_effects=True, vmem_limit_bytes=VMEM_LIMIT
        ),
    )(parts)


def local(tokens, expert_ids, gate_prob, w_gate, w_up, w_down):
    experts, tensors = lax.axis_size("expert"), lax.axis_size("tensor")
    me = lax.axis_index("expert")
    nx = ny = experts // 2
    nz = tensors // nx
    rows, columns = tokens.shape
    swap = [(e, e ^ 1) for e in range(experts)]
    core = lax.rem(me, 2)

    aux = jnp.concatenate(
        [expert_ids.astype(jnp.float32).T, gate_prob.T, jnp.zeros((4, rows), jnp.float32)], axis=0
    )
    blocks, table = gather(tokens, aux, nx, ny, nz)
    ids, prob = table[:, 0:2], table[:, 2:4]
    weight = jnp.sum(jnp.where(ids == me.astype(jnp.float32), prob, 0.0), axis=1)
    weight = weight.reshape(ny, 2, rows)

    def of_core(c):
        return lax.dynamic_index_in_dim(weight, c, 1, keepdims=False).reshape(ny * rows)

    mine = blocks.reshape(ny, tensors, rows, columns)
    mine = mine.transpose(0, 2, 1, 3).reshape(ny * rows, tensors * columns)
    theirs = lax.ppermute(mine, "expert", swap)

    def ffn(x, scale):
        gate = jnp.dot(x, w_gate[0], preferred_element_type=jnp.float32)
        up = jnp.dot(x, w_up[0], preferred_element_type=jnp.float32)
        hidden = (jax.nn.silu(gate) * up).astype(jnp.bfloat16)
        out = jnp.dot(hidden, w_down[0], preferred_element_type=jnp.float32)
        return out * scale[:, None]

    part_theirs = ffn(theirs, of_core(1 - core)).astype(jnp.bfloat16)
    arrived = lax.ppermute(part_theirs, "expert", swap)
    part_mine = ffn(mine, of_core(core))
    total = (part_mine + arrived.astype(jnp.float32)).astype(jnp.bfloat16)
    parts = total.reshape(ny, rows, tensors, columns).transpose(0, 2, 1, 3)
    return reduce_parts(parts.reshape(ny, nz, nx, rows, columns), nx, ny, nz)


def solution(mesh):
    return jax.shard_map(
        local,
        mesh=mesh,
        in_specs=(
            P("expert", "tensor"),
            P("expert", None),
            P("expert", None),
            P("expert", None, "tensor"),
            P("expert", None, "tensor"),
            P("expert", "tensor", None),
        ),
        out_specs=P("expert", "tensor"),
        check_vma=False,
    )
```

time: 348 us -> 257 us (0.74)
  waiting for transfers between devices: 234 us -> 10 us
  Pallas kernels: 0 us -> 155 us
  blocking collectives: 28.9 us -> 0 us
  local copies, waits for them, and re-layouts: 0.07 us -> 21.6 us
  between operations: 13.3 us -> 0.15 us
    pallas_call x0 -> x2, Pallas kernels: none -> 155 us  [the longest x1 93.2 us: reduce_parts(): pl.pallas_call(functools.partial(reduce_kernel, nx, ny, nz), out_shape=ja...]
    reduce_scatter x2 -> x0, waiting for transfers between devices: 136 us -> none  [the longest x1 117 us: local(): summed = lax.psum_scatter(total, 'tensor', scatter_dimension=1, tiled=True)]
    all_gather x1 -> x0, waiting for transfers between devices: 97.3 us -> none  [local(): mine = lax.all_gather(column, 'tensor', axis=1, tiled=True)]
    all_gather x3 -> x0, blocking collectives: 28.9 us -> none  [the longest x1 12.7 us: local(): lax.all_gather(tokens, 'expert', axis=0, tiled=True, axis_index_groups=ac...]
    unnamed x12 -> x19, local copies, waits for them, and re-layouts: 0.03 us -> 11.1 us
    reshape x2 -> x3, local copies, waits for them, and re-layouts: 0.04 us -> 10.4 us  [the longest x1 6.3 us: local(): mine = blocks.reshape(ny, tensors, rows, columns)]
    ppermute x1, waiting for transfers between devices: 0.01 us -> 10 us  [local(): theirs = lax.ppermute(mine, 'expert', swap)]
    dot_general x2, matrix products: 27.8 us -> 23.7 us  [ffn(): out = jnp.dot(hidden, w_down[0], preferred_element_type=jnp.float32)]
  transfers between devices with their start and end apart: 5 -> 2, of which waited for: 3 -> 1; matrix products, arithmetic and copies ran while one was open for 5% -> 8% of each run, Pallas kernels for 0% -> 0%
where the time goes in v1:
time: 257 us
  Pallas kernels  155 us (60%)
  matrix products  66.5 us (26%)
  local copies, waits for them, and re-layouts  21.6 us (8%)
  waiting for transfers between devices  10 us (4%)
    pallas_call x1, Pallas kernels, reduce_parts(): pl.pallas_call(functools.partial(reduce_kernel, nx, ny, nz), out_shape=ja...  93.2 us
    pallas_call x1, Pallas kernels, gather(): pl.pallas_call(functools.partial(gather_kernel, nx, ny, nz), out_shape=(j...  61.4 us
    dot_general x2, matrix products, ffn(): out = jnp.dot(hidden, w_down[0], preferred_element_type=jnp.float32)  23.7 us
    dot_general x2, matrix products, ffn(): gate = jnp.dot(x, w_gate[0], preferred_element_type=jnp.float32)  21.6 us
    dot_general x2, matrix products, ffn(): up = jnp.dot(x, w_up[0], preferred_element_type=jnp.float32)  21.2 us
    unnamed x19, local copies, waits for them, and re-layouts  11.1 us
    ppermute x1, waiting for transfers between devices, local(): theirs = lax.ppermute(mine, 'expert', swap)  10 us
    reshape x1, local copies, waits for them, and re-layouts, local(): mine = blocks.reshape(ny, tensors, rows, columns)  6.3 us
  transfers between devices with their start and end apart: 2, of which 1 were waited for; matrix products, arithmetic and copies ran while one was open for 8% of the time, Pallas kernels for 0%

profile of v1, /device:TPU:11, one launch (start us, length us, event | category | flops | bytes accessed | tf_op | source)
XLA Modules:
  0.0 256.7 jit_solution(1499795060061011208)
XLA Ops:
  0.0 0.7 convert_bitcast_fusion
  0.7 0.1 pad.2.clone
  0.8 1.3 maximum_maximum_fusion.aux_ref
  2.1 61.4 %shard_map.64 = (bf16[2,4,2,256,768]{4,3,2,1,0:T(8,128)(2,1)}, f32[4,8,256]{2,1,0:T(8,128)}) custom-call(bf16[256,768]{1,0:T(8,128)(2,1)} %own_ref.1, f32[8,256]{1,0:T(8,128)} %maximum_maximum_fusion.aux_ref), custom_call_target="tpu_custom_call" | custom-call | bytes 12582912 | tf_op jit(solution)/shard_map/pallas_call | solution.py:144
  63.5 6.3 %copy.8 = bf16[2,8,256,768]{3,1,2,0:T(8,128)(2,1)S(1)} copy(bf16[2,8,256,768]{3,2,1,0:T(8,128)(2,1)} %bitcast.45) | data formatting | bytes 12582912 | tf_op jit(solution)/shard_map/reshape | solution.py:317
  69.8 0.0 copy-start
  69.8 4.6 %copy.10 = bf16[64,8,8,768]{3,1,2,0:T(8,128)(2,1)} copy(bf16[64,8,8,768]{3,2,1,0:T(8,128)(2,1)S(1)} %bitcast.42) | data formatting | bytes 12582912
  74.5 1.3 collective-permute-start
  75.8 0.0 copy-done
  75.8 0.0 slice-start.3
  75.9 0.0 slice-start.4
  75.9 0.0 slice-start.5
  75.9 10.0 %collective-permute-done = bf16[512,6144]{1,0:T(8,128)(2,1)} collective-permute-done((bf16[512,6144]{1,0:T(8,128)(2,1)}, bf16[512,6144]{1,0:T(8,128)(2,1)}, u32[]{:S(2)}, u32[]{:S(2)}) %collective-permute-start) | collective-permute-done | bytes 6291488 | tf_op jit(solution)/shard_map/ppermute | solution.py:319
  85.9 12.4 %fusion.4 = f32[512,1024]{1,0:T(8,128)} fusion(bf16[512,6144]{1,0:T(8,128)(2,1)} %collective-permute-done, bf16[1,6144,1024]{2,1,0:T(8,128)(2,1)} %param.10), kind=kOutput, calls=%fused_computation.4 | convolution fusion | flops 6442450944 | bytes 20971520 | tf_op jit(solution)/shard_map/dot_general | solution.py:323
  98.4 0.0 slice-done.3
  98.4 0.0 slice-done.4
  98.4 0.0 slice-done.5
  98.4 0.0 slice-start
  98.4 0.0 slice-start.1
  98.4 9.8 %fusion.8 = f32[512,1024]{1,0:T(8,128)} fusion(bf16[512,6144]{1,0:T(8,128)(2,1)} %collective-permute-done, bf16[1,6144,1024]{2,1,0:T(8,128)(2,1)S(1)} %bitcast.53), kind=kOutput, calls=%fused_computation.8 | convolution fusion | flops 6442450944 | bytes 20971520 | tf_op jit(solution)/shard_map/dot_general | solution.py:322
  108.3 0.0 slice-start.2
  108.3 11.1 %multiply_convert_fusion = bf16[512,6144]{1,0:T(8,128)(2,1)S(1)} fusion(bf16[1,1024,6144]{2,1,0:T(8,128)(2,1)} %param.11, f32[512]{0:T(512)S(1)} %bitcast.49, f32[512,1024]{1,0:T(8,128)} %fusion.4, f32[512,1024]{1,0:T(8,128)} %fusion.8), kind=kOutput, calls=%fused_computation.13 | convolution fusion | flops 6451888128 | bytes 23070720 | tf_op jit(solution)/shard_map/dot_general | solution.py:325
  119.4 0.4 collective-permute-start.1
  119.8 0.0 slice-done
  119.8 0.0 slice-done.1
  119.8 0.0 slice-done.2
  119.8 8.7 %fusion.6 = f32[512,1024]{1,0:T(8,128)S(1)} fusion(bf16[512,6144]{1,0:T(8,128)(2,1)} %bitcast.14, bf16[1,6144,1024]{2,1,0:T(8,128)(2,1)S(1)} %bitcast.51), kind=kOutput, calls=%fused_computation.6 | convolution fusion | flops 6442450944 | bytes 20971520 | tf_op jit(solution)/shard_map/dot_general | solution.py:323
  128.6 11.8 %multiply_convert_fusion.2 = bf16[512,1024]{1,0:T(8,128)(2,1)S(1)} fusion(f32[512,1024]{1,0:T(8,128)S(1)} %fusion.6, bf16[512,6144]{1,0:T(8,128)(2,1)} %bitcast.14, bf16[1,6144,1024]{2,1,0:T(8,128)(2,1)} %param.9), kind=kOutput, calls=%fused_computation.15 | convolution fusion | flops 6445596672 | bytes 22020096 | tf_op jit(solution)/shard_map/dot_general | solution.py:322
  140.4 0.0 collective-permute-done.1
  140.4 0.0 copy-start.1
  140.4 2.6 %copy-done.1 = bf16[512,6144]{1,0:T(8,128)(2,1)} copy-done((bf16[512,6144]{1,0:T(8,128)(2,1)}, bf16[512,6144]{1,0:T(8,128)(2,1)S(1)}, u32[]{:S(2)}) %copy-start.1) | copy-done | bytes 6291480
  143.0 12.6 %add_convert_fusion = bf16[512,6144]{1,0:T(8,128)(2,1)S(1)} fusion(bf16[512,6144]{1,0:T(8,128)(2,1)} %copy-done.1, bf16[512,1024]{1,0:T(8,128)(2,1)S(1)} %multiply_convert_fusion.2, bf16[1,1024,6144]{2,1,0:T(8,128)(2,1)} %param.11, f32[512]{0:T(512)S(1)} %bitcast.48), kind=kOutput, calls=%fused_computation.12 | convolution fusion | flops 6455033856 | bytes 26216448 | tf_op jit(solution)/shard_map/dot_general | solution.py:325
  155.7 2.0 copy.11
  157.7 4.1 %copy.9 = bf16[2,256,8,768]{3,1,2,0:T(8,128)(2,1)} copy(bf16[2,256,8,768]{3,2,1,0:T(8,128)(2,1)S(1)} %bitcast.43) | data formatting | bytes 12582912 | tf_op jit(solution)/shard_map/reshape | solution.py:332
  161.7 93.2 %shard_map.65 = bf16[256,768]{1,0:T(8,128)(2,1)} custom-call(bf16[2,4,2,256,768]{4,3,2,1,0:T(8,128)(2,1)} %bitcast.44), custom_call_target="tpu_custom_call" | custom-call | bytes 12582912 | tf_op jit(solution)/shard_map/pallas_call | solution.py:269
  254.9 1.8 copy.13
  (6 shorter events, 0.1 us)
Async XLA Ops:
  69.8 6.0 %copy-start = (f32[4,8,256]{2,1,0:T(8,128)S(1)}, f32[4,8,256]{2,1,0:T(8,128)}, u32[]{:S(2)}) copy-start(f32[4,8,256]{2,1,0:T(8,128)} %get-tuple-element.8) | copy-start | bytes 98308
  74.5 11.5 %collective-permute-start = (bf16[512,6144]{1,0:T(8,128)(2,1)}, bf16[512,6144]{1,0:T(8,128)(2,1)}, u32[]{:S(2)}, u32[]{:S(2)}) collective-permute-start(bf16[512,6144]{1,0:T(8,128)(2,1)} %bitcast.14), channel_id=1, source_target_pairs={{0,8},{8,0},{16,24},{24,16},{1,9},{9,1},{17,25},{25,17},{2,10},{10... | collective-permute-start | bytes 18874376 | tf_op jit(solution)/shard_map/ppermute | solution.py:319
  75.8 22.5 %slice-start.3 = ((s8[12582912]{0:T(1024)(128)(4,1)}), s8[4194304]{0:T(1024)(128)(4,1)S(1)}, s32[]{:S(2)}) async-start(s8[12582912]{0:T(1024)(128)(4,1)} %bitcast.52), calls=%async_computation.3 | async-start | bytes 8388608
  75.9 22.5 %slice-start.4 = ((s8[12582912]{0:T(1024)(128)(4,1)}), s8[4194304]{0:T(1024)(128)(4,1)S(1)}, s32[]{:S(2)}) async-start(s8[12582912]{0:T(1024)(128)(4,1)} %bitcast.52), calls=%async_computation.4 | async-start | bytes 8388608
  75.9 22.5 %slice-start.5 = ((s8[12582912]{0:T(1024)(128)(4,1)}), s8[4194304]{0:T(1024)(128)(4,1)S(1)}, s32[]{:S(2)}) async-start(s8[12582912]{0:T(1024)(128)(4,1)} %bitcast.52), calls=%async_computation.5 | async-start | bytes 8388608
  98.4 21.4 %slice-start = ((s8[12582912]{0:T(1024)(128)(4,1)}), s8[4194304]{0:T(1024)(128)(4,1)S(1)}, s32[]{:S(2)}) async-start(s8[12582912]{0:T(1024)(128)(4,1)} %bitcast.50), calls=%async_computation | async-start | bytes 8388608
  98.4 21.4 %slice-start.1 = ((s8[12582912]{0:T(1024)(128)(4,1)}), s8[4194304]{0:T(1024)(128)(4,1)S(1)}, s32[]{:S(2)}) async-start(s8[12582912]{0:T(1024)(128)(4,1)} %bitcast.50), calls=%async_computation.1 | async-start | bytes 8388608
  108.3 11.6 %slice-start.2 = ((s8[12582912]{0:T(1024)(128)(4,1)}), s8[4194304]{0:T(1024)(128)(4,1)S(1)}, s32[]{:S(2)}) async-start(s8[12582912]{0:T(1024)(128)(4,1)} %bitcast.50), calls=%async_computation.2 | async-start | bytes 8388608
  119.4 21.0 %collective-permute-start.1 = (bf16[512,6144]{1,0:T(8,128)(2,1)S(1)}, bf16[512,6144]{1,0:T(8,128)(2,1)S(1)}, u32[]{:S(2)}, u32[]{:S(2)}) collective-permute-start(bf16[512,6144]{1,0:T(8,128)(2,1)S(1)} %multiply_convert_fusion), channel_id=1, source_target_pairs={{0,8},{8,0},{16,24},{24,16},{1,9},{9,1},{17,25},{25,17},{2,10},{10... | collective-permute-start | bytes 18874376 | tf_op jit(solution)/shard_map/ppermute | solution.py:329
  140.4 2.7 %copy-start.1 = (bf16[512,6144]{1,0:T(8,128)(2,1)}, bf16[512,6144]{1,0:T(8,128)(2,1)S(1)}, u32[]{:S(2)}) copy-start(bf16[512,6144]{1,0:T(8,128)(2,1)S(1)} %collective-permute-done.1) | copy-start | bytes 18874372

commit v2 on v1

--- a/solution.py
+++ b/solution.py
@@ -37,13 +37,38 @@
     )
 
 
+def is_flat(columns):
+    return columns % 128 == 0
+
+
+def slab(nx, columns, y, z, x, rows):
+    if not is_flat(columns):
+        return (y, z, x, rows)
+    if isinstance(x, slice):
+        start, width = z * (nx * columns), nx * columns
+    else:
+        start, width = (z * nx + x) * columns, columns
+    return (y, rows, pl.ds(pl.multiple_of(start, columns), width))
+
+
+def gathered(nx, ny, nz, rows, columns):
+    if is_flat(columns):
+        return (ny, rows, nz * nx * columns)
+    return (ny, nz, nx, rows, columns)
+
+
 def gather_kernel(
-    nx, ny, nz, own_ref, aux_ref, g_ref, all_ref, s1, r1, s2, r2, s3, r3, sa, ra, local_sem
+    nx, ny, nz, own_ref, aux_ref, g_ref, all_ref, s1, r1, s2, r2, s3, r3, s4, r4, sa, ra, local_sem
 ):
     e, x, y, z, core = place(nx, nz)
     experts = 2 * ny
     half = own_ref.shape[0] // 2
     t = z * nx + x
+    partner = (2 * y + 1 - core, t)
+    every = slice(None)
+
+    def at(side, ys, zs, xs, r):
+        return g_ref.at[(side, *slab(nx, own_ref.shape[1], ys, zs, xs, r))]
 
     def at_z(d):
         return (e, lax.rem(z + d, nz) * nx + x)
@@ -66,7 +91,7 @@
     rows = [pl.ds(0, half), pl.ds(half, half)]
     for h in range(2):
         keep = pltpu.make_async_copy(
-            own_ref.at[rows[h]], g_ref.at[y, z, x, rows[h]], local_sem.at[h]
+            own_ref.at[rows[h]], at(0, y, z, x, rows[h]), local_sem.at[h]
         )
         keep.start()
         waits.append((keep, False))
@@ -75,7 +100,7 @@
         for h in range(2):
             c = remote(
                 own_ref.at[rows[h]],
-                g_ref.at[y, z, x, rows[h]],
+                at(0, y, z, x, rows[h]),
                 (s1.at[h, d], r1.at[h, d]),
                 at_z(d),
             )
@@ -90,20 +115,20 @@
         c.start()
         aux.append(c)
 
-    second, third = {}, {}
+    second, third, fourth = {}, {}, {}
 
     def forward(d):
         zs = lax.rem(z + nz - d, nz)
         for h in range(2):
             if d:
                 first[h, d].wait_recv()
-                src = g_ref.at[y, zs, x, rows[h]]
+                src = at(0, y, zs, x, rows[h])
             else:
                 src = own_ref.at[rows[h]]
             n, to = ((nx, at_x), (ny, at_y))[h]
             for j in range(1, n):
                 c = remote(
-                    src, g_ref.at[y, zs, x, rows[h]], (s2.at[h, d, j], r2.at[h, d, j]), to(j)
+                    src, at(0, y, zs, x, rows[h]), (s2.at[h, d, j], r2.at[h, d, j]), to(j)
                 )
                 c.start()
                 second[h, d, j] = c
@@ -116,23 +141,50 @@
                 second[h, d, j].wait_recv()
             if d == 0:
                 waits[h][0].wait()
-            slab = g_ref.at[y, zs, :, rows[h]] if h == 0 else g_ref.at[:, zs, x, rows[h]]
+            line = (y, zs, every) if h == 0 else (every, zs, x)
+            held = at(0, *line, rows[h])
             for k in range(1, m):
-                c = remote(slab, slab, (s3.at[h, d, k], r3.at[h, d, k]), to(k))
+                c = remote(held, held, (s3.at[h, d, k], r3.at[h, d, k]), to(k))
                 c.start()
                 third[h, d, k] = c
+            hand_over(h, d, 0, line)
+
+    def hand_over(h, d, k, line):
+        if not is_flat(own_ref.shape[1]):
+            return
+        c = remote(
+            at(0, *line, rows[h]), at(1, *line, rows[h]), (s4.at[h, d, k], r4.at[h, d, k]), partner
+        )
+        c.start()
+        fourth[h, d, k] = c
+
+    def relay(d):
+        zs = lax.rem(z + nz - d, nz)
+        for k in range(1, max(nx, ny)):
+            for h in range(2):
+                if (h, d, k) in third:
+                    third[h, d, k].wait_recv()
+                    if h == 0:
+                        line = (lax.rem(y + ny - k, ny), zs, every)
+                    else:
+                        line = (every, zs, lax.rem(x + nx - k, nx))
+                    hand_over(h, d, k, line)
 
     forward(0)
     for d in range(1, nz):
         forward(d)
         spread(d - 1)
+        if d > 1:
+            relay(d - 2)
     spread(nz - 1)
-    for c in third.values():
+    for d in range(max(nz - 2, 0), nz):
+        relay(d)
+    for c in fourth.values():
         c.wait_recv()
     for c in aux:
         c.wait()
     waits[2][0].wait()
-    for c in [*first.values(), *second.values(), *third.values()]:
+    for c in [*first.values(), *second.values(), *third.values(), *fourth.values()]:
         c.wait_send()
 
 
@@ -144,7 +196,7 @@
     return pl.pallas_call(
         functools.partial(gather_kernel, nx, ny, nz),
         out_shape=(
-            jax.ShapeDtypeStruct((ny, nz, nx, rows, columns), tokens.dtype),
+            jax.ShapeDtypeStruct((1 + is_flat(columns), *gathered(nx, ny, nz, rows, columns)), tokens.dtype),
             jax.ShapeDtypeStruct((2 * ny, *aux.shape), aux.dtype),
         ),
         in_specs=[pl.BlockSpec(memory_space=pl.ANY)] * 2,
@@ -156,6 +208,8 @@
             dma((2, nz, n)),
             dma((2, nz, n)),
             dma((2, nz, n)),
+            dma((2, nz, n)),
+            dma((2, nz, n)),
             dma((2 * ny,)),
             dma((2 * ny,)),
             dma((3,)),
@@ -169,9 +223,18 @@
     nx, ny, nz, p_ref, o_ref, ya, xa, yb, xb, yc, xc, za, zb, s1, r1, s2, r2, s3, r3
 ):
     e, x, y, z, core = place(nx, nz)
-    half = o_ref.shape[0] // 2
+    half, columns = o_ref.shape[0] // 2, o_ref.shape[1]
     t = z * nx + x
     f32 = jnp.float32
+    every = slice(None)
+
+    def part(ys, zs, xs, r):
+        return slab(nx, columns, ys, zs, xs, r)
+
+    def entry(h, lead, i):
+        if h == 0 and is_flat(columns):
+            return (*lead, every, pl.ds(pl.multiple_of(i * columns, columns), columns))
+        return (*lead, i)
 
     def at_z(d):
         return (e, lax.rem(z + d, nz) * nx + x)
@@ -197,9 +260,9 @@
             n, to = ((ny, at_y), (nx, at_x))[h]
             for j in range(1, n):
                 if h == 0:
-                    src = p_ref.at[lax.rem(y + j, ny), zt, :, rows[h]]
+                    src = p_ref.at[part(lax.rem(y + j, ny), zt, every, rows[h])]
                 else:
-                    src = p_ref.at[:, zt, lax.rem(x + j, nx), rows[h]]
+                    src = p_ref.at[part(every, zt, lax.rem(x + j, nx), rows[h])]
                 c = remote(src, got[h].at[d, j - 1], (s1.at[h, d, j], r1.at[h, d, j]), to(j))
                 c.start()
                 one[h, d, j] = c
@@ -213,18 +276,18 @@
 
             def add(i, _, h=h, n=n):
                 if h == 0:
-                    total = p_ref[y, zt, i, rows[h]].astype(f32)
+                    total = p_ref[part(y, zt, i, rows[h])].astype(f32)
                 else:
-                    total = p_ref[i, zt, x, rows[h]].astype(f32)
+                    total = p_ref[part(i, zt, x, rows[h])].astype(f32)
                 for j in range(n - 1):
-                    total += got[h][d, j, i].astype(f32)
-                held[h][d, i] = total.astype(held[h].dtype)
+                    total += got[h][entry(h, (d, j), i)].astype(f32)
+                held[h][entry(h, (d,), i)] = total.astype(held[h].dtype)
                 return 0
 
             lax.fori_loop(0, m, add, 0)
             for k in range(1, m):
                 c = remote(
-                    held[h].at[d, lax.rem(at + k, m)],
+                    held[h].at[entry(h, (d,), lax.rem(at + k, m))],
                     last[h].at[d, k - 1],
                     (s2.at[h, d, k], r2.at[h, d, k]),
                     to(k),
@@ -237,7 +300,7 @@
             m, at = ((nx, x), (ny, y))[h]
             for k in range(1, m):
                 two[h, d, k].wait_recv()
-            total = held[h][d, at].astype(f32)
+            total = held[h][entry(h, (d,), at)].astype(f32)
             for k in range(m - 1):
                 total += last[h][d, k].astype(f32)
             za[h, d] = total.astype(za.dtype)
@@ -261,20 +324,20 @@
         c.wait_send()
 
 
-def reduce_parts(parts, nx, ny, nz):
-    rows, columns = parts.shape[-2:]
+def reduce_parts(parts, rows, columns, nx, ny, nz):
     half, n = rows // 2, max(nx, ny)
     kind = parts.dtype
     dma = pltpu.SemaphoreType.DMA
+    line = (half, nx * columns) if is_flat(columns) else (nx, half, columns)
     return pl.pallas_call(
         functools.partial(reduce_kernel, nx, ny, nz),
         out_shape=jax.ShapeDtypeStruct((rows, columns), kind),
         in_specs=[pl.BlockSpec(memory_space=pltpu.VMEM)],
         out_specs=pl.BlockSpec(memory_space=pltpu.VMEM),
         scratch_shapes=[
-            pltpu.VMEM((nz, ny - 1, nx, half, columns), kind),
+            pltpu.VMEM((nz, ny - 1, *line), kind),
             pltpu.VMEM((nz, nx - 1, ny, half, columns), kind),
-            pltpu.VMEM((nz, nx, half, columns), kind),
+            pltpu.VMEM((nz, *line), kind),
             pltpu.VMEM((nz, ny, half, columns), kind),
             pltpu.VMEM((nz, nx - 1, half, columns), kind),
             pltpu.VMEM((nz, ny - 1, half, columns), kind),
@@ -314,23 +377,31 @@
     def of_core(c):
         return lax.dynamic_index_in_dim(weight, c, 1, keepdims=False).reshape(ny * rows)
 
-    mine = blocks.reshape(ny, tensors, rows, columns)
-    mine = mine.transpose(0, 2, 1, 3).reshape(ny * rows, tensors * columns)
-    theirs = lax.ppermute(mine, "expert", swap)
-
-    def ffn(x, scale):
+    def up_half(x):
         gate = jnp.dot(x, w_gate[0], preferred_element_type=jnp.float32)
         up = jnp.dot(x, w_up[0], preferred_element_type=jnp.float32)
-        hidden = (jax.nn.silu(gate) * up).astype(jnp.bfloat16)
-        out = jnp.dot(hidden, w_down[0], preferred_element_type=jnp.float32)
-        return out * scale[:, None]
-
-    part_theirs = ffn(theirs, of_core(1 - core)).astype(jnp.bfloat16)
+        return (jax.nn.silu(gate) * up).astype(jnp.bfloat16)
+
+    if is_flat(columns):
+        hidden = up_half(blocks.reshape(2 * ny * rows, tensors * columns))
+        hidden_mine, hidden_theirs = hidden[: ny * rows], hidden[ny * rows :]
+    else:
+        mine = blocks.reshape(ny, tensors, rows, columns)
+        mine = mine.transpose(0, 2, 1, 3).reshape(ny * rows, tensors * columns)
+        theirs = lax.ppermute(mine, "expert", swap)
+        hidden_mine, hidden_theirs = up_half(mine), up_half(theirs)
+
+    def down(h, scale):
+        return jnp.dot(h, w_down[0], preferred_element_type=jnp.float32) * scale[:, None]
+
+    part_theirs = down(hidden_theirs, of_core(1 - core)).astype(jnp.bfloat16)
     arrived = lax.ppermute(part_theirs, "expert", swap)
-    part_mine = ffn(mine, of_core(core))
+    part_mine = down(hidden_mine, of_core(core))
     total = (part_mine + arrived.astype(jnp.float32)).astype(jnp.bfloat16)
-    parts = total.reshape(ny, rows, tensors, columns).transpose(0, 2, 1, 3)
-    return reduce_parts(parts.reshape(ny, nz, nx, rows, columns), nx, ny, nz)
+    parts = total.reshape(ny, rows, tensors * columns)
+    if not is_flat(columns):
+        parts = parts.reshape(ny, rows, nz, nx, columns).transpose(0, 2, 3, 1, 4)
+    return reduce_parts(parts, rows, columns, nx, ny, nz)
 
 
 def solution(mesh):

time: 257 us -> 228 us (0.89)
  local copies, waits for them, and re-layouts: 21.6 us -> 1.89 us
  matrix products: 66.5 us -> 53.9 us
  Pallas kernels: 155 us -> 158 us
    dot_general x6 -> x4, matrix products: 66.5 us -> 53.9 us  [the longest x2 20.5 us: down(): jnp.dot(h, w_down[0], preferred_element_type=jnp.float32) * scale[:, None]]
    reshape x2 -> x0, local copies, waits for them, and re-layouts: 10.4 us -> none  [the longest x1 6.3 us: local(): mine = blocks.reshape(ny, tensors, rows, columns)]
    ppermute x1, waiting for transfers between devices: 0.01 us -> 10.1 us  [local(): arrived = lax.ppermute(part_theirs, 'expert', swap)]
    ppermute x1 -> x0, waiting for transfers between devices: 10 us -> none  [local(): theirs = lax.ppermute(mine, 'expert', swap)]
    unnamed x19 -> x5, local copies, waits for them, and re-layouts: 11.1 us -> 1.78 us
    pallas_call x1, Pallas kernels: 61.4 us -> 65.2 us  [gather(): pl.pallas_call(functools.partial(gather_kernel, nx, ny, nz), out_shape=(j...]
  transfers between devices with their start and end apart: 2 -> 1, of which waited for: 1 -> 1; matrix products, arithmetic and copies ran while one was open for 8% -> 0% of each run, Pallas kernels for 0% -> 0%
where the time goes in v2:
time: 228 us; the launch traced here: 227 us
  Pallas kernels  158 us (69%)
  matrix products  53.9 us (24%)
  waiting for transfers between devices  10.1 us (4%)
  other arithmetic  2.89 us (1%)
    pallas_call x1, Pallas kernels, reduce_parts(): pl.pallas_call(functools.partial(reduce_kernel, nx, ny, nz), out_shape=ja...  93.2 us
    pallas_call x1, Pallas kernels, gather(): pl.pallas_call(functools.partial(gather_kernel, nx, ny, nz), out_shape=(j...  65.2 us
    dot_general x2, matrix products, down(): jnp.dot(h, w_down[0], preferred_element_type=jnp.float32) * scale[:, None]  20.5 us
    dot_general x1, matrix products, up_half(): up = jnp.dot(x, w_up[0], preferred_element_type=jnp.float32)  17.3 us
    dot_general x1, matrix products, up_half(): gate = jnp.dot(x, w_gate[0], preferred_element_type=jnp.float32)  16.2 us
    ppermute x1, waiting for transfers between devices, local(): arrived = lax.ppermute(part_theirs, 'expert', swap)  10.1 us
  transfers between devices with their start and end apart: 1, of which 1 were waited for; matrix products, arithmetic and copies ran while one was open for 0% of the time, Pallas kernels for 0%

profile of v2, /device:TPU:11, one launch (start us, length us, event | category | flops | bytes accessed | tf_op | source)
XLA Modules:
  0.0 227.3 jit_solution(8103786799186336172)
XLA Ops:
  0.0 0.7 convert_bitcast_fusion
  0.7 0.1 pad.2.clone
  0.8 1.3 maximum_maximum_fusion.aux_ref
  2.1 65.2 %shard_map.64 = (bf16[2,2,256,6144]{3,2,1,0:T(8,128)(2,1)}, f32[4,8,256]{2,1,0:T(8,128)}) custom-call(bf16[256,768]{1,0:T(8,128)(2,1)} %own_ref.1, f32[8,256]{1,0:T(8,128)} %maximum_maximum_fusion.aux_ref), custom_call_target="tpu_custom_call" | custom-call | bytes 12582912 | tf_op jit(solution)/shard_map/pallas_call | solution.py:196
  67.3 0.9 fusion.16
  68.1 0.0 copy-start
  68.2 17.3 %fusion.4 = f32[1024,1024]{1,0:T(8,128)S(1)} fusion(bf16[1024,6144]{1,0:T(8,128)(2,1)} %bitcast.30, bf16[1,6144,1024]{2,1,0:T(8,128)(2,1)} %param.10), kind=kOutput, calls=%fused_computation.4 | convolution fusion | flops 12884901888 | bytes 29360128 | tf_op jit(solution)/shard_map/dot_general | solution.py:382
  85.4 0.0 copy-done
  85.4 16.2 %multiply_convert_fusion.1 = bf16[1024,1024]{1,0:T(8,128)(2,1)S(1)} fusion(f32[1024,1024]{1,0:T(8,128)S(1)} %fusion.4, bf16[1024,6144]{1,0:T(8,128)(2,1)} %bitcast.31, bf16[1,6144,1024]{2,1,0:T(8,128)(2,1)S(1)} %copy-done), kind=kOutput, calls=%fused_computation.10 | convolution fusion | flops 12891193344 | bytes 31457280 | tf_op jit(solution)/shard_map/dot_general | solution.py:381
  101.7 0.0 copy-start.1
  101.7 11.7 %multiply_convert_fusion = bf16[512,6144]{1,0:T(8,128)(2,1)S(1)} fusion(bf16[1,1024,6144]{2,1,0:T(8,128)(2,1)} %param.11, f32[512]{0:T(512)S(1)} %bitcast.29, bf16[1024,1024]{1,0:T(8,128)(2,1)S(1)} %multiply_convert_fusion.1), kind=kOutput, calls=%fused_computation.9 | convolution fusion | flops 6448742400 | bytes 19924992 | tf_op jit(solution)/shard_map/dot_general | solution.py:395
  113.4 0.1 collective-permute-start
  113.5 10.1 %collective-permute-done = bf16[512,6144]{1,0:T(8,128)(2,1)S(1)} collective-permute-done((bf16[512,6144]{1,0:T(8,128)(2,1)S(1)}, bf16[512,6144]{1,0:T(8,128)(2,1)S(1)}, u32[]{:S(2)}, u32[]{:S(2)}) %collective-permute-start) | collective-permute-done | bytes 6291488 | tf_op jit(solution)/shard_map/ppermute | solution.py:398
  123.6 0.0 copy-done.1
  123.6 8.8 %add_convert_fusion = bf16[512,6144]{1,0:T(8,128)(2,1)} fusion(bf16[512,6144]{1,0:T(8,128)(2,1)S(1)} %collective-permute-done, bf16[1,1024,6144]{2,1,0:T(8,128)(2,1)S(1)} %copy-done.1, f32[512]{0:T(512)S(1)} %bitcast.28, bf16[1024,1024]{1,0:T(8,128)(2,1)S(1)} %multiply_convert_fusion.1), kind=kOutput, calls=%fused_computation.8 | convolution fusion | flops 6455033856 | bytes 26216448 | tf_op jit(solution)/shard_map/dot_general | solution.py:395
  132.4 93.2 %shard_map.65 = bf16[256,768]{1,0:T(8,128)(2,1)} custom-call(bf16[2,256,6144]{2,1,0:T(8,128)(2,1)} %bitcast.26), custom_call_target="tpu_custom_call" | custom-call | bytes 12582912 | tf_op jit(solution)/shard_map/pallas_call | solution.py:332
  225.5 1.8 copy.8
  (3 shorter events, 0.0 us)
Async XLA Ops:
  68.1 17.3 %copy-start = (bf16[1,6144,1024]{2,1,0:T(8,128)(2,1)S(1)}, bf16[1,6144,1024]{2,1,0:T(8,128)(2,1)}, u32[]{:S(2)}) copy-start(bf16[1,6144,1024]{2,1,0:T(8,128)(2,1)} %param.9) | copy-start | bytes 37748740
  101.7 21.9 %copy-start.1 = (bf16[1,1024,6144]{2,1,0:T(8,128)(2,1)S(1)}, bf16[1,1024,6144]{2,1,0:T(8,128)(2,1)}, u32[]{:S(2)}) copy-start(bf16[1,1024,6144]{2,1,0:T(8,128)(2,1)} %param.11) | copy-start | bytes 37748740
  113.4 10.2 %collective-permute-start = (bf16[512,6144]{1,0:T(8,128)(2,1)S(1)}, bf16[512,6144]{1,0:T(8,128)(2,1)S(1)}, u32[]{:S(2)}, u32[]{:S(2)}) collective-permute-start(bf16[512,6144]{1,0:T(8,128)(2,1)S(1)} %multiply_convert_fusion), channel_id=1, source_target_pairs={{0,8},{8,0},{16,24},{24,16},{1,9},{9,1},{17,25},{25,17},{2,10},{10... | collective-permute-start | bytes 18874376 | tf_op jit(solution)/shard_map/ppermute | solution.py:398
